TPU v7x, 32 devices: a whole 2x2x4 slice. The times are simulated.
32 devices in a mesh: parts: 2 (over y), patch: 4 (over z), sub: 2 (over x), rep: 2 (over core).
Axes of the slice: x: 2, y: 2, z: 4, core: 2. Of those that a mesh axis runs over, the one named last changes fastest.
Arguments:
- sky_maps: bfloat16 [4, 8, 16384], P(('parts', 'rep'), None, ('patch', 'sub')), parts along dimension 0, may hold values from -6 to 6
- nb_fine: int32 [8, 16384], P(None, ('patch', 'sub')), may hold values from -128 to 128, as said below
- w_fine: float32 [8, 16384], P(None, ('patch', 'sub')), may hold values from 0.25 to 1
- nb_coarse: int32 [8, 1024], P(None, ('patch', 'sub')), may hold values from -128 to 128, as said below
- w_coarse: float32 [8, 1024], P(None, ('patch', 'sub')), may hold values from 0.25 to 1
- conv_fine: bfloat16 [48, 32], replicated, may hold values from -0.875 to 0.875
- conv_coarse: bfloat16 [192, 128], replicated, may hold values from -0.4375 to 0.4375
- head: bfloat16 [160, 8], replicated, may hold values from -0.5 to 0.5
- cotangent: bfloat16 [4, 8, 16384], P(('parts', 'rep'), None, ('patch', 'sub')), parts along dimension 0, may hold values from -6 to 6
Outputs:
- prediction: bfloat16 [4, 8, 16384], P(('parts', 'rep'), None, ('patch', 'sub')), parts along dimension 0
- grad_fine: float32 [96, 32], P('parts'), parts along dimension 0
- grad_coarse: float32 [384, 128], P('parts'), parts along dimension 0
- grad_head: float32 [320, 8], P('parts'), parts along dimension 0
There are 2 independent parts, one for each index of `parts`. A program takes and returns all parts, laid end to end along the dimension named above; an argument that names none is the same for every part. Nothing has to cross between parts.
Inputs may be any that keep to these rules, and one draw needn't show every extreme that they name: `nb_fine`: offsets in the cyclic nested order of the 16384 fine pixels; some are exactly 128 and some exactly -128. `nb_coarse`: offsets in the cyclic nested order of the 1024 coarse pixels; some are exactly 128 and some exactly -128.
All inputs are finite; a program needn't handle non-finite values.
Results may differ from a plain program's by a relative error of at most 0.012.
Values may be sent and summed in bfloat16 or wider, within the bound.
A program may use at most 64 MiB of HBM per device.

v0:
```python
from functools import partial
import math

import jax
import jax.numpy as jnp
from jax import lax
from jax.sharding import PartitionSpec as P

FEAT_FINE = 32
ORDER = 6
MAPS_DEV = 1
HALO = 128


def extended_2(block, sides, width):
    for axis, dim in sides:
        count = lax.axis_size(axis)
        forward = [(i, i + 1) for i in range(count - 1)]
        forward.append((count - 1, 0))
        backward = [(target, source) for source, target in forward]
        low = lax.ppermute(
            lax.slice_in_dim(block, block.shape[dim] - width, None, axis=dim), axis, forward
        )
        high = lax.ppermute(lax.slice_in_dim(block, 0, width, axis=dim), axis, backward)
        block = jnp.concatenate([low, block, high], axis=dim)
    return block


def shifted(x, axis, by):
    length = lax.axis_size(axis)
    return lax.ppermute(x, axis, [(i, (i + by) % length) for i in range(length)])


def relax(values, nearby, degree):
    return (degree * values - nearby) * 0.125 - values


def slot_sum(values, index, weight):
    nearby = weight[0] * values[:, index[0]]
    for column in range(1, 8):
        nearby = nearby + weight[column] * values[:, index[column]]
    return nearby


def fine_step(field, index, weight, degree):
    extended = extended_2(field, ((("patch", "sub"), 1),), HALO)
    return relax(field, slot_sum(extended, index, weight), degree)


def coarse_step(field, index, weight, degree):
    extended = extended_2(field, ((("patch", "sub"), 1),), HALO)
    return relax(field, slot_sum(extended, index, weight), degree)


def coarse_adjoint(field, index, weight, degree):
    rows, pixels = field.shape
    spread = jnp.zeros((rows, pixels + 2 * HALO), jnp.float32)
    for column in range(8):
        spread = spread.at[:, index[column]].add(weight[column] * field)
    from_next = shifted(spread[:, :HALO], ("patch", "sub"), -1)
    from_prev = shifted(spread[:, pixels + HALO :], ("patch", "sub"), 1)
    interior = spread[:, HALO : HALO + pixels]
    interior = interior.at[:, pixels - HALO :].add(from_next)
    interior = interior.at[:, :HALO].add(from_prev)
    return (degree * field - interior) * 0.125 - field


def chebyshev(field, operator):
    polys = [field, operator(field)]
    for level in range(2, ORDER):
        polys.append(2.0 * operator(polys[-1]) - polys[-2])
    return jnp.stack(polys)


def slope(pre_act):
    sigmoid_value = jax.nn.sigmoid(pre_act)
    return sigmoid_value * (1.0 + pre_act * (1.0 - sigmoid_value))


def on_device(
    sky_maps, nb_fine, w_fine, nb_coarse, w_coarse, conv_fine, conv_coarse, head, cotangent
):
    map_count, channel_count, pixels = sky_maps.shape
    coarse_pixels = pixels // 16
    cycle_count = lax.axis_size(("patch", "sub"))
    pixel_total = pixels * cycle_count
    fine_width = conv_fine.shape[1]
    coarse_width = conv_coarse.shape[1]
    out_width = head.shape[1]
    highest = lax.Precision.HIGHEST
    fine_local = jnp.arange(pixels, dtype=jnp.int32)[None, :] + nb_fine + HALO
    fine_degree = jnp.sum(w_fine, axis=0)
    fine_field = sky_maps.astype(jnp.float32).reshape(map_count * channel_count, pixels)
    fine_polys = chebyshev(
        fine_field, partial(fine_step, index=fine_local, weight=w_fine, degree=fine_degree)
    )
    fine_stack = fine_polys.reshape(ORDER, map_count, channel_count, pixels).astype(jnp.bfloat16)
    fine_pre = jnp.einsum(
        "kco,kmcp->mop",
        conv_fine.reshape(ORDER, channel_count, fine_width),
        fine_stack,
        preferred_element_type=jnp.float32,
    )
    fine_hidden = jax.nn.silu(fine_pre).astype(jnp.bfloat16)
    pooled = (
        jnp.sum(
            fine_hidden.astype(jnp.float32).reshape(map_count, fine_width, coarse_pixels, 16),
            axis=3,
        )
        * 0.0625
    )
    coarse_local = jnp.arange(coarse_pixels, dtype=jnp.int32)[None, :] + nb_coarse + HALO
    coarse_degree = jnp.sum(w_coarse, axis=0)
    coarse_field = pooled.reshape(map_count * fine_width, coarse_pixels)
    coarse_polys = chebyshev(
        coarse_field,
        partial(coarse_step, index=coarse_local, weight=w_coarse, degree=coarse_degree),
    )
    coarse_stack = coarse_polys.reshape(ORDER, map_count, fine_width, coarse_pixels).astype(
        jnp.bfloat16
    )
    conv_blocks = conv_coarse.reshape(ORDER, fine_width, coarse_width)
    coarse_pre = jnp.einsum(
        "kco,kmcp->mop", conv_blocks, coarse_stack, preferred_element_type=jnp.float32
    )
    coarse_hidden = jax.nn.silu(coarse_pre).astype(jnp.bfloat16)
    head_fine = head[:FEAT_FINE]
    head_coarse = head[FEAT_FINE:]
    upward = jnp.einsum(
        "co,mcp->mop", head_coarse, coarse_hidden, preferred_element_type=jnp.float32
    )
    result = jnp.einsum(
        "co,mcp->mop", head_fine, fine_hidden, preferred_element_type=jnp.float32
    ) + jnp.repeat(upward, 16, axis=2)
    prediction = result.astype(jnp.bfloat16)
    loss_scale = 1.0 / math.sqrt(pixel_total * MAPS_DEV * lax.axis_size("rep"))
    signal = (cotangent.astype(jnp.float32) * loss_scale).astype(jnp.bfloat16)
    pooled_signal = jnp.sum(
        signal.astype(jnp.float32).reshape(map_count, out_width, coarse_pixels, 16), axis=3
    )
    grad_top = jnp.einsum("mcp,mop->co", fine_hidden, signal, preferred_element_type=jnp.float32)
    grad_low = jnp.einsum(
        "mcp,mop->co", coarse_hidden.astype(jnp.float32), pooled_signal, precision=highest
    )
    grad_top, grad_low = lax.psum((grad_top, grad_low), ("patch", "sub", "rep"))
    coarse_back = jnp.einsum(
        "co,mop->mcp", head_coarse.astype(jnp.float32), pooled_signal, precision=highest
    )
    coarse_delta = (coarse_back * slope(coarse_pre)).astype(jnp.bfloat16)
    grad_two = jnp.einsum(
        "kmcp,mop->kco", coarse_stack, coarse_delta, preferred_element_type=jnp.float32
    ).reshape(ORDER * fine_width, coarse_width)
    grad_two = lax.psum(grad_two, ("patch", "sub", "rep"))
    coarse_adj = jnp.einsum(
        "kco,mop->kmcp", conv_blocks, coarse_delta, preferred_element_type=jnp.float32
    )
    adjoint = [
        coarse_adj[level].reshape(map_count * fine_width, coarse_pixels) for level in range(ORDER)
    ]
    for level in range(ORDER - 1, 1, -1):
        adjoint[level - 1] = adjoint[level - 1] + 2.0 * coarse_adjoint(
            adjoint[level], coarse_local, w_coarse, coarse_degree
        )
        adjoint[level - 2] = adjoint[level - 2] - adjoint[level]
    pooled_grad = adjoint[0] + coarse_adjoint(adjoint[1], coarse_local, w_coarse, coarse_degree)
    pooled_grad = pooled_grad.reshape(map_count, fine_width, coarse_pixels)
    fine_back = jnp.einsum(
        "co,mop->mcp", head_fine, signal, preferred_element_type=jnp.float32
    ) + jnp.repeat(pooled_grad * 0.0625, 16, axis=2)
    fine_delta = (fine_back * slope(fine_pre)).astype(jnp.bfloat16)
    grad_one = jnp.einsum(
        "kmcp,mop->kco", fine_stack, fine_delta, preferred_element_type=jnp.float32
    ).reshape(ORDER * channel_count, fine_width)
    grad_one = lax.psum(grad_one, ("patch", "sub", "rep"))
    return (prediction, grad_one, grad_two, jnp.concatenate([grad_top, grad_low], axis=0))


def solution(mesh):
    return jax.shard_map(
        on_device,
        mesh=mesh,
        in_specs=(
            P(("parts", "rep"), None, ("patch", "sub")),
            P(None, ("patch", "sub")),
            P(None, ("patch", "sub")),
            P(None, ("patch", "sub")),
            P(None, ("patch", "sub")),
            P(),
            P(),
            P(),
            P(("parts", "rep"), None, ("patch", "sub")),
        ),
        out_specs=(
            P(("parts", "rep"), None, ("patch", "sub")),
            P("parts", None),
            P("parts", None),
            P("parts", None),
        ),
        check_vma=False,
    )
```

profile of v0, /device:TPU:0, one launch (start us, length us, event | category | flops | bytes accessed | tf_op | source)
XLA Modules:
  0.0 618.7 jit_solution(3758156584030114232)
XLA Ops:
  8.1 6.0 collective-permute-start.1
  27.0 5.5 gather_fusion.7
  32.8 5.5 gather_fusion.6
  38.5 5.5 gather_fusion.5
  44.3 5.5 gather_fusion.4
  50.1 5.5 gather_fusion.3
  55.8 5.5 gather_fusion.2
  61.6 5.5 gather_fusion.1
  67.4 5.5 gather_fusion
  79.4 4.9 collective-permute-done.2
  84.7 7.6 %gather_fusion.15 = f32[2048,8]{1,0:T(8,128)} fusion(f32[8,2304]{0,1:T(8,128)S(1)} %copy.466, s32[2048]{0:T(1024)S(1)} %get-tuple-element.338), kind=kCustom, calls=%fused_computation.15 | custom fusion | bytes 139264 | tf_op jit(solution)/shard_map/gather | solution.py:41
  92.3 7.6 %gather_fusion.14 = f32[2048,8]{1,0:T(8,128)} fusion(f32[8,2304]{0,1:T(8,128)S(1)} %copy.466, s32[2048]{0:T(1024)S(1)} %get-tuple-element.339), kind=kCustom, calls=%fused_computation.14 | custom fusion | bytes 139264 | tf_op jit(solution)/shard_map/gather | solution.py:41
  99.9 7.6 %gather_fusion.13 = f32[2048,8]{1,0:T(8,128)} fusion(f32[8,2304]{0,1:T(8,128)S(1)} %copy.466, s32[2048]{0:T(1024)S(1)} %get-tuple-element.340), kind=kCustom, calls=%fused_computation.13 | custom fusion | bytes 139264 | tf_op jit(solution)/shard_map/gather | solution.py:41
  107.4 7.5 %gather_fusion.12 = f32[2048,8]{1,0:T(8,128)} fusion(f32[8,2304]{0,1:T(8,128)S(1)} %copy.466, s32[2048]{0:T(1024)S(1)} %get-tuple-element.341), kind=kCustom, calls=%fused_computation.12 | custom fusion | bytes 139264 | tf_op jit(solution)/shard_map/gather | solution.py:41
  115.0 7.6 %gather_fusion.11 = f32[2048,8]{1,0:T(8,128)} fusion(f32[8,2304]{0,1:T(8,128)S(1)} %copy.466, s32[2048]{0:T(1024)S(1)} %get-tuple-element.342), kind=kCustom, calls=%fused_computation.11 | custom fusion | bytes 139264 | tf_op jit(solution)/shard_map/gather | solution.py:41
  122.5 7.6 %gather_fusion.10 = f32[2048,8]{1,0:T(8,128)} fusion(f32[8,2304]{0,1:T(8,128)S(1)} %copy.466, s32[2048]{0:T(1024)S(1)} %get-tuple-element.343), kind=kCustom, calls=%fused_computation.10 | custom fusion | bytes 139264 | tf_op jit(solution)/shard_map/gather | solution.py:41
  130.1 5.5 gather_fusion.9
  135.6 5.5 gather_fusion.8
  158.3 7.6 %gather_fusion.23 = f32[2048,8]{1,0:T(8,128)} fusion(f32[8,2304]{0,1:T(8,128)S(1)} %copy.482, s32[2048]{0:T(1024)S(1)} %get-tuple-element.338), kind=kCustom, calls=%fused_computation.23 | custom fusion | bytes 139264 | tf_op jit(solution)/shard_map/gather | solution.py:41
  165.9 7.6 %gather_fusion.22 = f32[2048,8]{1,0:T(8,128)} fusion(f32[8,2304]{0,1:T(8,128)S(1)} %copy.482, s32[2048]{0:T(1024)S(1)} %get-tuple-element.339), kind=kCustom, calls=%fused_computation.22 | custom fusion | bytes 139264 | tf_op jit(solution)/shard_map/gather | solution.py:41
  173.5 7.6 %gather_fusion.21 = f32[2048,8]{1,0:T(8,128)} fusion(f32[8,2304]{0,1:T(8,128)S(1)} %copy.482, s32[2048]{0:T(1024)S(1)} %copy-done.36), kind=kCustom, calls=%fused_computation.21 | custom fusion | bytes 139264 | tf_op jit(solution)/shard_map/gather | solution.py:41
  181.0 7.5 %gather_fusion.20 = f32[2048,8]{1,0:T(8,128)} fusion(f32[8,2304]{0,1:T(8,128)S(1)} %copy.482, s32[2048]{0:T(1024)S(1)} %get-tuple-element.341), kind=kCustom, calls=%fused_computation.20 | custom fusion | bytes 139264 | tf_op jit(solution)/shard_map/gather | solution.py:41
  188.6 7.6 %gather_fusion.19 = f32[2048,8]{1,0:T(8,128)} fusion(f32[8,2304]{0,1:T(8,128)S(1)} %copy.482, s32[2048]{0:T(1024)S(1)} %copy-done.44), kind=kCustom, calls=%fused_computation.19 | custom fusion | bytes 139264 | tf_op jit(solution)/shard_map/gather | solution.py:41
  196.1 7.6 %gather_fusion.18 = f32[2048,8]{1,0:T(8,128)} fusion(f32[8,2304]{0,1:T(8,128)S(1)} %copy.482, s32[2048]{0:T(1024)S(1)} %copy-done.40), kind=kCustom, calls=%fused_computation.18 | custom fusion | bytes 139264 | tf_op jit(solution)/shard_map/gather | solution.py:41
  203.7 5.5 gather_fusion.17
  209.1 6.4 %gather_fusion.16 = f32[2048,8]{1,0:T(8,128)S(1)} fusion(f32[8,2304]{0,1:T(8,128)S(1)} %copy.482, s32[2048]{0:T(1024)} %copy-done.47), kind=kCustom, calls=%fused_computation.16 | custom fusion | bytes 139264 | tf_op jit(solution)/shard_map/gather | solution.py:39
  233.3 7.6 %gather_fusion.31 = f32[2048,8]{1,0:T(8,128)} fusion(f32[8,2304]{0,1:T(8,128)S(1)} %copy.498, s32[2048]{0:T(1024)S(1)} %get-tuple-element.338), kind=kCustom, calls=%fused_computation.31 | custom fusion | bytes 139264 | tf_op jit(solution)/shard_map/gather | solution.py:41
  240.9 7.6 %gather_fusion.30 = f32[2048,8]{1,0:T(8,128)} fusion(f32[8,2304]{0,1:T(8,128)S(1)} %copy.498, s32[2048]{0:T(1024)S(1)} %get-tuple-element.339), kind=kCustom, calls=%fused_computation.30 | custom fusion | bytes 139264 | tf_op jit(solution)/shard_map/gather | solution.py:41
  248.5 7.6 %gather_fusion.29 = f32[2048,8]{1,0:T(8,128)} fusion(f32[8,2304]{0,1:T(8,128)S(1)} %copy.498, s32[2048]{0:T(1024)S(1)} %copy-done.37), kind=kCustom, calls=%fused_computation.29 | custom fusion | bytes 139264 | tf_op jit(solution)/shard_map/gather | solution.py:41
  256.0 7.5 %gather_fusion.28 = f32[2048,8]{1,0:T(8,128)} fusion(f32[8,2304]{0,1:T(8,128)S(1)} %copy.498, s32[2048]{0:T(1024)S(1)} %get-tuple-element.341), kind=kCustom, calls=%fused_computation.28 | custom fusion | bytes 139264 | tf_op jit(solution)/shard_map/gather | solution.py:41
  263.6 7.6 %gather_fusion.27 = f32[2048,8]{1,0:T(8,128)} fusion(f32[8,2304]{0,1:T(8,128)S(1)} %copy.498, s32[2048]{0:T(1024)S(1)} %copy-done.45), kind=kCustom, calls=%fused_computation.27 | custom fusion | bytes 139264 | tf_op jit(solution)/shard_map/gather | solution.py:41
  271.2 7.6 %gather_fusion.26 = f32[2048,8]{1,0:T(8,128)} fusion(f32[8,2304]{0,1:T(8,128)S(1)} %copy.498, s32[2048]{0:T(1024)S(1)} %copy-done.41), kind=kCustom, calls=%fused_computation.26 | custom fusion | bytes 139264 | tf_op jit(solution)/shard_map/gather | solution.py:41
  278.7 5.5 gather_fusion.25
  284.2 5.5 gather_fusion.24
  306.9 5.5 gather_fusion.39
  312.4 5.5 gather_fusion.38
  317.9 7.6 %gather_fusion.37 = f32[2048,8]{1,0:T(8,128)} fusion(f32[8,2304]{0,1:T(8,128)S(1)} %copy.514, s32[2048]{0:T(1024)S(1)} %copy-done.38), kind=kCustom, calls=%fused_computation.37 | custom fusion | bytes 139264 | tf_op jit(solution)/shard_map/gather | solution.py:41
  325.5 7.6 %gather_fusion.36 = f32[2048,8]{1,0:T(8,128)} fusion(f32[8,2304]{0,1:T(8,128)S(1)} %copy.514, s32[2048]{0:T(1024)S(1)} %get-tuple-element.341), kind=kCustom, calls=%fused_computation.36 | custom fusion | bytes 139264 | tf_op jit(solution)/shard_map/gather | solution.py:41
  333.1 7.6 %gather_fusion.35 = f32[2048,8]{1,0:T(8,128)} fusion(f32[8,2304]{0,1:T(8,128)S(1)} %copy.514, s32[2048]{0:T(1024)S(1)} %copy-done.46), kind=kCustom, calls=%fused_computation.35 | custom fusion | bytes 139264 | tf_op jit(solution)/shard_map/gather | solution.py:41
  340.6 7.6 %gather_fusion.34 = f32[2048,8]{1,0:T(8,128)} fusion(f32[8,2304]{0,1:T(8,128)S(1)} %copy.514, s32[2048]{0:T(1024)S(1)} %copy-done.42), kind=kCustom, calls=%fused_computation.34 | custom fusion | bytes 139264 | tf_op jit(solution)/shard_map/gather | solution.py:41
  348.2 7.5 %gather_fusion.33 = f32[2048,8]{1,0:T(8,128)} fusion(f32[8,2304]{0,1:T(8,128)S(1)} %copy.514, s32[2048]{0:T(1024)S(1)} %copy-done.53), kind=kCustom, calls=%fused_computation.33 | custom fusion | bytes 139264 | tf_op jit(solution)/shard_map/gather | solution.py:41
  355.7 7.6 %gather_fusion.32 = f32[2048,8]{1,0:T(8,128)} fusion(f32[8,2304]{0,1:T(8,128)S(1)} %copy.514, s32[2048]{0:T(1024)S(1)} %copy-done.49), kind=kCustom, calls=%fused_computation.32 | custom fusion | bytes 139264 | tf_op jit(solution)/shard_map/gather | solution.py:39
  464.2 4.8 collective-permute-start.22
  482.3 4.8 collective-permute-start.24
  500.7 4.8 collective-permute-start.26
  518.9 4.8 collective-permute-start.28
  526.7 58.1 %all-reduce = (f32[48,32]{0,1:T(8,128)}, f32[128,8]{0,1:T(8,128)S(1)}, f32[32,8]{0,1:T(8,128)S(1)}) all-reduce(f32[48,32]{0,1:T(8,128)S(1)} %fusion.8, f32[128,8]{0,1:T(8,128)S(1)} %fusion.138, f32[32,8]{0,1:T(8,128)S(1)} %fusion.14), channel_id=1, replica_groups=mesh['parts'=2,'patch'=4,'sub'=2,'rep'=2] {'patch','sub','rep'}, use_global_device_ids=true, to_apply=%region_44.45 | all-reduce | flops 2816 | bytes 22528 | tf_op jit(solution)/shard_map/psum | solution.py:174
  585.5 24.3 %all-reduce.3.cloned.1.call-done = f32[192,128]{1,0:T(8,128)} async-done(((f32[192,128]{1,0:T(8,128)}), f32[192,128]{1,0:T(8,128)}) %all-reduce.3.cloned.1.call-update) | async-done | bytes 98320 | tf_op jit(solution)/shard_map/psum | solution.py:153
  (575 shorter events, 219.7 us)
Async XLA Ops:
  7.2 426.3 %copy-start = (bf16[192,128]{1,0:T(8,128)(2,1)S(1)}, bf16[192,128]{1,0:T(8,128)(2,1)}, u32[]{:S(2)}) copy-start(bf16[192,128]{1,0:T(8,128)(2,1)} %param.55) | copy-start | bytes 147460
  7.2 602.7 %all-reduce.3.cloned.1.call-start = ((), (), s32[]{:S(2)}) async-start(), calls=%async_computation | async-start | bytes 196608 | tf_op jit(solution)/shard_map/psum | solution.py:153
  8.1 18.4 %collective-permute-start.1 = (f32[8,128]{1,0:T(8,128)S(1)}, f32[8,128]{1,0:T(8,128)S(1)}, u32[]{:S(2)}, u32[]{:S(2)}) collective-permute-start(f32[8,128]{1,0:T(8,128)S(1)} %get-tuple-element.279), channel_id=1, source_target_pairs={{2,0},{4,2},{6,4},{8,6},{10,8},{12,10},{14,12},{0,14},{3,1},{5,3},... | collective-permute-start | bytes 12296 | tf_op jit(solution)/shard_map/ppermute | solution.py:24
  14.1 12.4 %collective-permute-start = (f32[8,128]{1,0:T(8,128)S(1)}, f32[8,128]{1,0:T(8,128)S(1)}, u32[]{:S(2)}, u32[]{:S(2)}) collective-permute-start(f32[8,128]{1,0:T(8,128)S(1)} %get-tuple-element.278), channel_id=1, source_target_pairs={{0,2},{2,4},{4,6},{6,8},{8,10},{10,12},{12,14},{14,0},{1,3},{3,5},... | collective-permute-start | bytes 12296 | tf_op jit(solution)/shard_map/ppermute | solution.py:21
  20.8 79.1 %copy-start.35 = (s32[2048]{0:T(1024)}, s32[2048]{0:T(1024)S(1)}, u32[]{:S(2)}) copy-start(s32[2048]{0:T(1024)S(1)} %get-tuple-element.340) | copy-start | bytes 24580
  20.8 94.2 %copy-start.43 = (s32[2048]{0:T(1024)}, s32[2048]{0:T(1024)S(1)}, u32[]{:S(2)}) copy-start(s32[2048]{0:T(1024)S(1)} %get-tuple-element.342) | copy-start | bytes 24580
  20.8 101.7 %copy-start.39 = (s32[2048]{0:T(1024)}, s32[2048]{0:T(1024)S(1)}, u32[]{:S(2)}) copy-start(s32[2048]{0:T(1024)S(1)} %get-tuple-element.343) | copy-start | bytes 24580
  20.8 109.3 %copy-start.50 = (s32[2048]{0:T(1024)}, s32[2048]{0:T(1024)S(1)}, u32[]{:S(2)}) copy-start(s32[2048]{0:T(1024)S(1)} %get-tuple-element.344) | copy-start | bytes 24580
  20.8 114.7 %copy-start.47 = (s32[2048]{0:T(1024)}, s32[2048]{0:T(1024)S(1)}, u32[]{:S(2)}) copy-start(s32[2048]{0:T(1024)S(1)} %get-tuple-element.345) | copy-start | bytes 24580
  73.3 6.1 collective-permute-start.3
  78.0 6.3 %collective-permute-start.2 = (f32[8,128]{1,0:T(8,128)S(1)}, f32[8,128]{1,0:T(8,128)S(1)}, u32[]{:S(2)}, u32[]{:S(2)}) collective-permute-start(f32[8,128]{1,0:T(8,128)S(1)} %get-tuple-element.260), channel_id=1, source_target_pairs={{0,2},{2,4},{4,6},{6,8},{8,10},{10,12},{12,14},{14,0},{1,3},{3,5},... | collective-permute-start | bytes 12296 | tf_op jit(solution)/shard_map/ppermute | solution.py:21
  151.5 3.7 collective-permute-start.5
  151.6 6.4 %collective-permute-start.4 = (f32[8,128]{1,0:T(8,128)S(1)}, f32[8,128]{1,0:T(8,128)S(1)}, u32[]{:S(2)}, u32[]{:S(2)}) collective-permute-start(f32[8,128]{1,0:T(8,128)S(1)} %get-tuple-element.258), channel_id=1, source_target_pairs={{0,2},{2,4},{4,6},{6,8},{8,10},{10,12},{12,14},{14,0},{1,3},{3,5},... | collective-permute-start | bytes 12296 | tf_op jit(solution)/shard_map/ppermute | solution.py:21
  158.3 30.3 %copy-start.44 = (s32[2048]{0:T(1024)S(1)}, s32[2048]{0:T(1024)}, u32[]{:S(2)}) copy-start(s32[2048]{0:T(1024)} %copy-done.43) | copy-start | bytes 24580
  165.9 30.2 %copy-start.40 = (s32[2048]{0:T(1024)S(1)}, s32[2048]{0:T(1024)}, u32[]{:S(2)}) copy-start(s32[2048]{0:T(1024)} %copy-done.39) | copy-start | bytes 24580
  173.5 30.2 %copy-start.51 = (s32[2048]{0:T(1024)S(1)}, s32[2048]{0:T(1024)}, u32[]{:S(2)}) copy-start(s32[2048]{0:T(1024)} %copy-done.50) | copy-start | bytes 24580
  226.0 3.7 collective-permute-start.7
  226.1 6.8 %collective-permute-start.6 = (f32[8,128]{1,0:T(8,128)S(1)}, f32[8,128]{1,0:T(8,128)S(1)}, u32[]{:S(2)}, u32[]{:S(2)}) collective-permute-start(f32[8,128]{1,0:T(8,128)S(1)} %get-tuple-element.256), channel_id=1, source_target_pairs={{0,2},{2,4},{4,6},{6,8},{8,10},{10,12},{12,14},{14,0},{1,3},{3,5},... | collective-permute-start | bytes 12296 | tf_op jit(solution)/shard_map/ppermute | solution.py:21
  233.3 30.3 %copy-start.45 = (s32[2048]{0:T(1024)S(1)}, s32[2048]{0:T(1024)}, u32[]{:S(2)}) copy-start(s32[2048]{0:T(1024)} %copy-done.43) | copy-start | bytes 24580
  240.9 30.2 %copy-start.41 = (s32[2048]{0:T(1024)S(1)}, s32[2048]{0:T(1024)}, u32[]{:S(2)}) copy-start(s32[2048]{0:T(1024)} %copy-done.39) | copy-start | bytes 24580
  248.5 30.2 %copy-start.52 = (s32[2048]{0:T(1024)S(1)}, s32[2048]{0:T(1024)}, u32[]{:S(2)}) copy-start(s32[2048]{0:T(1024)} %copy-done.50) | copy-start | bytes 24580
  256.0 28.1 %copy-start.48 = (s32[2048]{0:T(1024)S(1)}, s32[2048]{0:T(1024)}, u32[]{:S(2)}) copy-start(s32[2048]{0:T(1024)} %copy-done.47) | copy-start | bytes 24580
  300.1 3.7 collective-permute-start.9
  300.2 6.4 %collective-permute-start.8 = (f32[8,128]{1,0:T(8,128)S(1)}, f32[8,128]{1,0:T(8,128)S(1)}, u32[]{:S(2)}, u32[]{:S(2)}) collective-permute-start(f32[8,128]{1,0:T(8,128)S(1)} %get-tuple-element.254), channel_id=1, source_target_pairs={{0,2},{2,4},{4,6},{6,8},{8,10},{10,12},{12,14},{14,0},{1,3},{3,5},... | collective-permute-start | bytes 12296 | tf_op jit(solution)/shard_map/ppermute | solution.py:21
  306.9 26.1 %copy-start.46 = (s32[2048]{0:T(1024)S(1)}, s32[2048]{0:T(1024)}, u32[]{:S(2)}) copy-start(s32[2048]{0:T(1024)} %copy-done.43) | copy-start | bytes 24580
  312.4 28.2 %copy-start.42 = (s32[2048]{0:T(1024)S(1)}, s32[2048]{0:T(1024)}, u32[]{:S(2)}) copy-start(s32[2048]{0:T(1024)} %copy-done.39) | copy-start | bytes 24580
  317.9 30.3 %copy-start.53 = (s32[2048]{0:T(1024)S(1)}, s32[2048]{0:T(1024)}, u32[]{:S(2)}) copy-start(s32[2048]{0:T(1024)} %copy-done.50) | copy-start | bytes 24580
  325.5 30.3 %copy-start.49 = (s32[2048]{0:T(1024)S(1)}, s32[2048]{0:T(1024)}, u32[]{:S(2)}) copy-start(s32[2048]{0:T(1024)} %copy-done.47) | copy-start | bytes 24580
  370.8 3.8 collective-permute-start.11
  370.8 6.5 %collective-permute-start.10 = (f32[32,128]{1,0:T(8,128)S(1)}, f32[32,128]{1,0:T(8,128)S(1)}, u32[]{:S(2)}, u32[]{:S(2)}) collective-permute-start(f32[32,128]{1,0:T(8,128)S(1)} %broadcast_multiply_fusion), channel_id=1, source_target_pairs={{0,2},{2,4},{4,6},{6,8},{8,10},{10,12},{12,14},{14,0},{1,3},{3,5},... | collective-permute-start | bytes 49160 | tf_op jit(solution)/shard_map/ppermute | solution.py:21
  383.3 3.8 collective-permute-start.13
  383.4 6.5 %collective-permute-start.12 = (f32[32,128]{1,0:T(8,128)S(1)}, f32[32,128]{1,0:T(8,128)S(1)}, u32[]{:S(2)}, u32[]{:S(2)}) collective-permute-start(f32[32,128]{1,0:T(8,128)S(1)} %fusion.250), channel_id=1, source_target_pairs={{0,2},{2,4},{4,6},{6,8},{8,10},{10,12},{12,14},{14,0},{1,3},{3,5},... | collective-permute-start | bytes 49160 | tf_op jit(solution)/shard_map/ppermute | solution.py:21
  395.8 3.8 collective-permute-start.15
  395.9 6.5 %collective-permute-start.14 = (f32[32,128]{1,0:T(8,128)S(1)}, f32[32,128]{1,0:T(8,128)S(1)}, u32[]{:S(2)}, u32[]{:S(2)}) collective-permute-start(f32[32,128]{1,0:T(8,128)S(1)} %fusion.240), channel_id=1, source_target_pairs={{0,2},{2,4},{4,6},{6,8},{8,10},{10,12},{12,14},{14,0},{1,3},{3,5},... | collective-permute-start | bytes 49160 | tf_op jit(solution)/shard_map/ppermute | solution.py:21
  408.3 3.8 collective-permute-start.17
  408.4 6.5 %collective-permute-start.16 = (f32[32,128]{1,0:T(8,128)S(1)}, f32[32,128]{1,0:T(8,128)S(1)}, u32[]{:S(2)}, u32[]{:S(2)}) collective-permute-start(f32[32,128]{1,0:T(8,128)S(1)} %fusion.228), channel_id=1, source_target_pairs={{0,2},{2,4},{4,6},{6,8},{8,10},{10,12},{12,14},{14,0},{1,3},{3,5},... | collective-permute-start | bytes 49160 | tf_op jit(solution)/shard_map/ppermute | solution.py:21
  420.8 3.8 collective-permute-start.19
  420.9 6.7 %collective-permute-start.18 = (f32[32,128]{1,0:T(8,128)S(1)}, f32[32,128]{1,0:T(8,128)S(1)}, u32[]{:S(2)}, u32[]{:S(2)}) collective-permute-start(f32[32,128]{1,0:T(8,128)S(1)} %fusion.216), channel_id=1, source_target_pairs={{0,2},{2,4},{4,6},{6,8},{8,10},{10,12},{12,14},{14,0},{1,3},{3,5},... | collective-permute-start | bytes 49160 | tf_op jit(solution)/shard_map/ppermute | solution.py:21
  445.9 6.5 %collective-permute-start.21 = (f32[32,128]{1,0:T(8,128)S(1)}, f32[32,128]{1,0:T(8,128)S(1)}, u32[]{:S(2)}, u32[]{:S(2)}) collective-permute-start(f32[32,128]{1,0:T(8,128)S(1)} %copy.677), channel_id=1, source_target_pairs={{0,2},{2,4},{4,6},{6,8},{8,10},{10,12},{12,14},{14,0},{1,3},{3,5},... | collective-permute-start | bytes 49160 | tf_op jit(solution)/shard_map/ppermute | solution.py:31
  446.0 6.4 %collective-permute-start.20 = (f32[32,128]{1,0:T(8,128)S(1)}, f32[32,128]{1,0:T(8,128)S(1)}, u32[]{:S(2)}, u32[]{:S(2)}) collective-permute-start(f32[32,128]{1,0:T(8,128)S(1)} %copy.676), channel_id=1, source_target_pairs={{0,14},{2,0},{4,2},{6,4},{8,6},{10,8},{12,10},{14,12},{1,15},{3,1}... | collective-permute-start | bytes 49160 | tf_op jit(solution)/shard_map/ppermute | solution.py:31
  464.1 6.5 %collective-permute-start.23 = (f32[32,128]{1,0:T(8,128)S(1)}, f32[32,128]{1,0:T(8,128)S(1)}, u32[]{:S(2)}, u32[]{:S(2)}) collective-permute-start(f32[32,128]{1,0:T(8,128)S(1)} %copy.680), channel_id=1, source_target_pairs={{0,2},{2,4},{4,6},{6,8},{8,10},{10,12},{12,14},{14,0},{1,3},{3,5},... | collective-permute-start | bytes 49160 | tf_op jit(solution)/shard_map/ppermute | solution.py:31
  464.2 6.5 %collective-permute-start.22 = (f32[32,128]{1,0:T(8,128)S(1)}, f32[32,128]{1,0:T(8,128)S(1)}, u32[]{:S(2)}, u32[]{:S(2)}) collective-permute-start(f32[32,128]{1,0:T(8,128)S(1)} %copy.679), channel_id=1, source_target_pairs={{0,14},{2,0},{4,2},{6,4},{8,6},{10,8},{12,10},{14,12},{1,15},{3,1}... | collective-permute-start | bytes 49160 | tf_op jit(solution)/shard_map/ppermute | solution.py:31
  482.2 6.5 %collective-permute-start.25 = (f32[32,128]{1,0:T(8,128)S(1)}, f32[32,128]{1,0:T(8,128)S(1)}, u32[]{:S(2)}, u32[]{:S(2)}) collective-permute-start(f32[32,128]{1,0:T(8,128)S(1)} %copy.683), channel_id=1, source_target_pairs={{0,2},{2,4},{4,6},{6,8},{8,10},{10,12},{12,14},{14,0},{1,3},{3,5},... | collective-permute-start | bytes 49160 | tf_op jit(solution)/shard_map/ppermute | solution.py:31
  482.3 6.5 %collective-permute-start.24 = (f32[32,128]{1,0:T(8,128)S(1)}, f32[32,128]{1,0:T(8,128)S(1)}, u32[]{:S(2)}, u32[]{:S(2)}) collective-permute-start(f32[32,128]{1,0:T(8,128)S(1)} %copy.682), channel_id=1, source_target_pairs={{0,14},{2,0},{4,2},{6,4},{8,6},{10,8},{12,10},{14,12},{1,15},{3,1}... | collective-permute-start | bytes 49160 | tf_op jit(solution)/shard_map/ppermute | solution.py:31
  500.6 6.6 %collective-permute-start.27 = (f32[32,128]{1,0:T(8,128)S(1)}, f32[32,128]{1,0:T(8,128)S(1)}, u32[]{:S(2)}, u32[]{:S(2)}) collective-permute-start(f32[32,128]{1,0:T(8,128)S(1)} %copy.686), channel_id=1, source_target_pairs={{0,2},{2,4},{4,6},{6,8},{8,10},{10,12},{12,14},{14,0},{1,3},{3,5},... | collective-permute-start | bytes 49160 | tf_op jit(solution)/shard_map/ppermute | solution.py:31
  500.7 6.5 %collective-permute-start.26 = (f32[32,128]{1,0:T(8,128)S(1)}, f32[32,128]{1,0:T(8,128)S(1)}, u32[]{:S(2)}, u32[]{:S(2)}) collective-permute-start(f32[32,128]{1,0:T(8,128)S(1)} %copy.685), channel_id=1, source_target_pairs={{0,14},{2,0},{4,2},{6,4},{8,6},{10,8},{12,10},{14,12},{1,15},{3,1}... | collective-permute-start | bytes 49160 | tf_op jit(solution)/shard_map/ppermute | solution.py:31
  518.8 6.5 %collective-permute-start.29 = (f32[32,128]{1,0:T(8,128)S(1)}, f32[32,128]{1,0:T(8,128)S(1)}, u32[]{:S(2)}, u32[]{:S(2)}) collective-permute-start(f32[32,128]{1,0:T(8,128)S(1)} %copy.689), channel_id=1, source_target_pairs={{0,2},{2,4},{4,6},{6,8},{8,10},{10,12},{12,14},{14,0},{1,3},{3,5},... | collective-permute-start | bytes 49160 | tf_op jit(solution)/shard_map/ppermute | solution.py:31
  518.9 6.5 %collective-permute-start.28 = (f32[32,128]{1,0:T(8,128)S(1)}, f32[32,128]{1,0:T(8,128)S(1)}, u32[]{:S(2)}, u32[]{:S(2)}) collective-permute-start(f32[32,128]{1,0:T(8,128)S(1)} %copy.688), channel_id=1, source_target_pairs={{0,14},{2,0},{4,2},{6,4},{8,6},{10,8},{12,10},{14,12},{1,15},{3,1}... | collective-permute-start | bytes 49160 | tf_op jit(solution)/shard_map/ppermute | solution.py:31
  (84 other events, 479.8 us)
Sparse Core Ops, SparseCore 0:
  524.0 85.8 all-reduce.2
where the time goes:
time: 627 us; the launch traced here: 619 us
  local copies, waits for them, and re-layouts  354 us (56%)
  waiting for transfers between devices  68.5 us (11%)
  other arithmetic  66.6 us (11%)
  blocking collectives  58.1 us (9%)
  starting transfers between devices  52.2 us (8%)
  between operations  16.4 us (3%)
    gather x140, local copies, waits for them, and re-layouts, slot_sum(): nearby = nearby + weight[column] * values[:, index[column]]  300 us
    psum x1, blocking collectives, on_device(): grad_one = lax.psum(grad_one, ('patch', 'sub', 'rep'))  58.1 us
    scatter-add x40, other arithmetic, coarse_adjoint(): spread = spread.at[:, index[column]].add(weight[column] * field)  53.4 us
    gather x20, local copies, waits for them, and re-layouts, slot_sum(): nearby = weight[0] * values[:, index[0]]  35.5 us
    ppermute x10, waiting for transfers between devices, extended_2(): lax.ppermute(lax.slice_in_dim(block, block.shape[dim] - width, None, axis...  27.7 us
    psum x1, waiting for transfers between devices, on_device(): grad_two = lax.psum(grad_two, ('patch', 'sub', 'rep'))  24.3 us
    ppermute x10, starting transfers between devices, shifted(): lax.ppermute(x, axis, [(i, (i + by) % length) for i in range(length)])  24.2 us
    ppermute x10, starting transfers between devices, extended_2(): lax.ppermute(lax.slice_in_dim(block, block.shape[dim] - width, None, axis...  16.7 us
  transfers between devices with their start and end apart: 31, of which 24 were waited for; matrix products, arithmetic and copies ran while one was open for 3% of the time, Pallas kernels for 0%

commit v1 on v0

v1 whole, which is shorter than its diff:
```python
from functools import partial
import math

import jax
import jax.numpy as jnp
from jax import lax
from jax.experimental import pallas as pl
from jax.experimental.pallas import tpu as pltpu
from jax.sharding import PartitionSpec as P

ORDER = 6
LANES = 128
REACH = ORDER - 1
MESH = pl.DeviceIdType.MESH
F32 = jnp.float32
BF16 = jnp.bfloat16


def dot(a, b, dims=((1,), (0,))):
    return lax.dot_general(a, b, (dims, ((), ())), preferred_element_type=F32)


def split2(x):
    high = x.astype(BF16)
    low = (x - high.astype(F32)).astype(BF16)
    return high, low


def gate(v):
    return 0.5 * jnp.tanh(0.5 * v) + 0.5


def window_of(count):
    full = count <= 4 * REACH + 2
    held = count if full else 4 * REACH + 2
    offsets = [d if d <= held // 2 else d - held for d in range(held)]
    peers = [p for p in range(1, held) if full or abs(offsets[p]) <= 2 * REACH]
    return full, held, offsets, peers


def kernel(
    ring, reps, scale, sky, nbf, wf, nbc, wc, conv_f, conv_c, head, cot,
    pred, out_fine, out_coarse, out_head,
    field, nb, wt, idx8, w8, deg, stack, pool, cg, pg, mat, gc, gc_in, pack, pack_in, total, all_in,
    halo_send, halo_recv, cg_send, cg_recv, pg_send, pg_recv, rep_send, rep_recv, all_send, all_recv,
):
    patches, subs = ring
    count = patches * subs
    full, held, offsets, peers = window_of(count)
    me = lax.axis_index("patch") * subs + lax.axis_index("sub")
    rep = lax.axis_index("rep")
    blocks = sky.shape[2] // LANES
    first, last = REACH, REACH + blocks

    def at(d):
        q = lax.rem(me + (d % count), count)
        return {"patch": lax.div(q, subs), "sub": lax.rem(q, subs)}

    partner = {"rep": lax.rem(rep + 1, reps)}
    barrier = pltpu.get_barrier_semaphore()
    for p in peers:
        pl.semaphore_signal(barrier, inc=1, device_id=at(offsets[p]), device_id_type=MESH)
    if full:
        pl.semaphore_signal(barrier, inc=1, device_id=partner, device_id_type=MESH)

    for b in range(blocks):
        rows = slice((first + b) * 8, (first + b + 1) * 8)
        lanes = slice(b * LANES, (b + 1) * LANES)
        field[0, rows, :] = sky[0, :, lanes].astype(F32)
        nb[rows, :] = nbf[:, lanes]
        wt[rows, :] = wf[:, lanes] * 0.125

    pl.semaphore_wait(barrier, len(peers) + (1 if full else 0))

    def push(src, dst, ssem, rsem, to):
        copy = pltpu.make_async_remote_copy(
            src_ref=src, dst_ref=dst, send_sem=ssem, recv_sem=rsem, device_id=to, device_id_type=MESH
        )
        copy.start()
        return copy

    halos = []
    for n, (ref, width) in enumerate(((field.at[0], REACH), (nb, REACH - 1), (wt, REACH - 1))):
        size = width * 8
        skip = (REACH - width) * 8
        halos.append(push(
            ref.at[pl.ds(last * 8 - size, size)], ref.at[pl.ds(skip, size)],
            halo_send.at[2 * n], halo_recv.at[2 * n], at(1)))
        halos.append(push(
            ref.at[pl.ds(first * 8, size)], ref.at[pl.ds(last * 8, size)],
            halo_send.at[2 * n + 1], halo_recv.at[2 * n + 1], at(-1)))

    pixel = lax.broadcasted_iota(jnp.int32, pool.shape, 0)
    coarse = lax.broadcasted_iota(jnp.int32, pool.shape, 1)
    pool[...] = jnp.where((pixel >> 4) == coarse, 1.0, 0.0).astype(BF16)
    signal = (cot[0].astype(F32) * scale).astype(BF16)
    pooled_signal = dot(signal, pool[...])
    cg[0, 0:8, :] = nbc[...].astype(F32)
    cg[0, 8:16, :] = wc[...] * 0.125
    cg[0, 16:24, :] = pooled_signal
    gathers = []
    for p in peers:
        back = (held - p) % held
        gathers.append(push(cg.at[0], cg.at[back], cg_send.at[p], cg_recv.at[back], at(offsets[p])))

    def spread_slots(b0, b1):
        shape = (b1 - b0, 8, LANES)
        rows = slice(b0 * 8, b1 * 8)
        lane = lax.broadcasted_iota(jnp.int32, ((b1 - b0) * 8, LANES), 1)
        near_nb = nb[rows, :].reshape(shape)
        near_w = wt[rows, :].reshape(shape)
        acc = None
        for j in range(8):
            offs = jnp.broadcast_to(near_nb[:, j : j + 1, :], shape).reshape((b1 - b0) * 8, LANES)
            wide = jnp.broadcast_to(near_w[:, j : j + 1, :], shape).reshape((b1 - b0) * 8, LANES)
            idx8[j, rows, :] = offs + lane
            w8[j, rows, :] = wide
            acc = wide if acc is None else acc + wide
        deg[rows, :] = acc - 1.0

    def level(k, b0, b1):
        rows = slice(b0 * 8, b1 * 8)
        lo = field[k - 1, slice(b0 * 8 - 8, b1 * 8 - 8), :]
        mid = field[k - 1, rows, :]
        hi = field[k - 1, slice(b0 * 8 + 8, b1 * 8 + 8), :]
        near = None
        for j in range(8):
            index = idx8[j, rows, :]
            source = index & (LANES - 1)
            g = jnp.where(
                index < 0,
                jnp.take_along_axis(lo, source, axis=1, mode="promise_in_bounds"),
                jnp.where(
                    index >= LANES,
                    jnp.take_along_axis(hi, source, axis=1, mode="promise_in_bounds"),
                    jnp.take_along_axis(mid, source, axis=1, mode="promise_in_bounds"),
                ),
            )
            term = w8[j, rows, :] * g
            near = term if near is None else near + term
        lap = deg[rows, :] * mid - near
        field[k, rows, :] = lap if k == 1 else 2.0 * lap - field[k - 2, rows, :]

    spread_slots(first, last)
    for k in range(1, ORDER):
        level(k, first + k, last - k)
    for copy in halos:
        copy.wait()
    spread_slots(1, first)
    spread_slots(last, last + REACH - 1)
    for k in range(1, ORDER):
        level(k, k, first + k)
        level(k, last - k, last + REACH - k)
    for b in range(blocks):
        tile = field[:, slice((first + b) * 8, (first + b + 1) * 8), :]
        stack[:, slice(b * LANES, (b + 1) * LANES)] = tile.reshape(ORDER * 8, LANES).astype(BF16)

    fine_pre = dot(conv_f[...], stack[...], ((0,), (0,)))
    fine_gate = gate(fine_pre)
    hidden = (fine_pre * fine_gate).astype(BF16)
    pg[0] = dot(hidden, pool[...]) * 0.0625
    pooled_gathers = []
    for p in peers:
        back = (held - p) % held
        pooled_gathers.append(
            push(pg.at[0], pg.at[back], pg_send.at[p], pg_recv.at[back], at(offsets[p])))

    grad_top = dot(signal, hidden, ((1,), (1,)))
    fine_slope = fine_gate * (1.0 + fine_pre * (1.0 - fine_gate))
    head_fine = head[0:32, :]
    head_coarse = head[32:160, :]
    direct = dot(head_fine, signal)
    result_fine = dot(head_fine, hidden, ((0,), (0,)))

    for copy in gathers:
        copy.wait()
    if not full:
        cg[held // 2] = cg[0]
    source = lax.broadcasted_iota(jnp.int32, (3 * LANES, LANES), 0)
    lane = lax.broadcasted_iota(jnp.int32, (8, LANES), 1)
    degrees = []
    for t in range(held):
        offs = cg[t, 0:8, :].astype(jnp.int32) + lane + LANES
        weight = cg[t, 8:16, :]
        block = None
        for j in range(8):
            term = jnp.where(offs[j : j + 1, :] == source, weight[j : j + 1, :], 0.0)
            block = term if block is None else block + term
        u, side = t // 2, t % 2
        cols = slice(side * LANES, (side + 1) * LANES)
        mat[u, slice(side * LANES, (side + 3) * LANES), cols] = block.astype(BF16)
        empty = 3 * LANES if side == 0 else 0
        mat[u, slice(empty, empty + LANES), cols] = jnp.zeros((LANES, LANES), BF16)
        degrees.append(jnp.sum(weight, axis=0, keepdims=True) - 1.0)
    degree = jnp.concatenate(degrees, axis=1)
    signals = jnp.concatenate([cg[t, 16:24, :] for t in range(held)], axis=1)
    sig_high, sig_low = split2(signals)
    coarse_back = dot(head_coarse, sig_high) + dot(head_coarse, sig_low)

    for copy in pooled_gathers:
        copy.wait()
    if not full:
        pg[held // 2] = pg[0]

    wide = held * LANES

    def forward(x):
        rows = x.shape[0]
        high, low = split2(x)
        both = jnp.concatenate([high, low], axis=0)
        both = jnp.concatenate([both[:, wide - LANES :], both, both[:, :LANES]], axis=1)
        parts = []
        for u in range(held // 2):
            got = dot(both[:, 2 * u * LANES : (2 * u + 4) * LANES], mat[u])
            parts.append(got[:rows] + got[rows:])
        return degree * x - jnp.concatenate(parts, axis=1)

    def adjoint(x):
        rows = x.shape[0]
        high, low = split2(x)
        both = jnp.concatenate([high, low], axis=0)
        sums = [None] * held
        for u in range(held // 2):
            got = dot(both[:, 2 * u * LANES : (2 * u + 2) * LANES], mat[u], ((1,), (1,)))
            got = got[:rows] + got[rows:]
            for i in range(4):
                s = (2 * u - 1 + i) % held
                piece = got[:, i * LANES : (i + 1) * LANES]
                sums[s] = piece if sums[s] is None else sums[s] + piece
        return degree * x - jnp.concatenate(sums, axis=1)

    poly = [jnp.concatenate([pg[t] for t in range(held)], axis=1)]
    poly.append(forward(poly[0]))
    for k in range(2, ORDER):
        poly.append(2.0 * forward(poly[-1]) - poly[-2])
    coarse_stack = jnp.concatenate(poly, axis=0).astype(BF16)
    coarse_pre = dot(conv_c[...], coarse_stack, ((0,), (0,)))
    coarse_gate = gate(coarse_pre)
    coarse_hidden = (coarse_pre * coarse_gate).astype(BF16)
    coarse_delta = (
        coarse_back * (coarse_gate * (1.0 + coarse_pre * (1.0 - coarse_gate)))
    ).astype(BF16)
    coarse_adj = dot(conv_c[...], coarse_delta)
    adj = [coarse_adj[32 * k : 32 * (k + 1)] for k in range(ORDER)]
    for k in range(ORDER - 1, 1, -1):
        adj[k - 1] = adj[k - 1] + 2.0 * adjoint(adj[k])
        adj[k - 2] = adj[k - 2] - adj[k]
    pooled_grad = (adj[0] + adjoint(adj[1]))[:, :LANES] * 0.0625

    pool_t = ((1,), (1,))
    grad_high, grad_low_part = split2(pooled_grad)
    raised = dot(jnp.concatenate([grad_high, grad_low_part], axis=0), pool[...], pool_t)
    fine_delta = ((direct + raised[:32] + raised[32:]) * fine_slope).astype(BF16)
    grad_fine = dot(stack[...], fine_delta, pool_t)

    pack[:, 0:32] = grad_fine[0:16]
    pack[:, 32:64] = grad_fine[16:32]
    pack[:, 64:96] = grad_fine[32:48]
    pack[0:8, 96:128] = grad_top
    pack[8:16, 96:128] = jnp.zeros((8, 32), F32)
    if full:
        pair = push(pack, pack_in, rep_send.at[0], rep_recv.at[0], partner)

    span = slice(0, wide if full else LANES)
    gc[0:192, :] = dot(coarse_stack[:, span], coarse_delta[:, span], pool_t)
    gc[192:200, :] = dot(sig_high[:, span], coarse_hidden[:, span], pool_t) + dot(
        sig_low[:, span], coarse_hidden[:, span], pool_t)

    if full:
        pair.wait()
        total[0] = pack[...] + pack_in[...]
        spreads = []
        for p in peers:
            back = (held - p) % held
            spreads.append(
                push(total.at[0], total.at[back], all_send.at[p], all_recv.at[back], at(offsets[p])))
        pair_coarse = push(gc, gc_in, rep_send.at[1], rep_recv.at[1], partner)

    upward = dot(head_coarse, coarse_hidden[:, :LANES], ((0,), (0,)))
    up_high, up_low = split2(upward)
    result = result_fine + dot(up_high, pool[...], pool_t) + dot(up_low, pool[...], pool_t)
    pred[0] = result.astype(BF16)

    if full:
        pair_coarse.wait()
        sums = gc[...] + gc_in[...]
        for copy in spreads:
            copy.wait()
        whole = total[0]
        for t in range(1, held):
            whole = whole + total[t]
    else:
        sums = gc[...]
        whole = pack[...]
    out_coarse[...] = sums[0:192]
    out_fine[0:16, :] = whole[:, 0:32]
    out_fine[16:32, :] = whole[:, 32:64]
    out_fine[32:48, :] = whole[:, 64:96]
    out_head[0:32, :] = jnp.transpose(whole[0:8, 96:128])
    out_head[32:160, :] = jnp.transpose(sums[192:200])


def on_device(ring, reps, *args):
    sky, conv_f, conv_c, head = args[0], args[5], args[6], args[7]
    pixels = sky.shape[2]
    count = ring[0] * ring[1]
    full, held, _, _ = window_of(count)
    rows = (pixels // LANES + 2 * REACH) * 8
    scale = 1.0 / math.sqrt(pixels * count * sky.shape[0] * reps)
    dma = pltpu.SemaphoreType.DMA
    vmem = pl.BlockSpec(memory_space=pltpu.VMEM)
    result = pl.pallas_call(
        partial(kernel, ring, reps, scale),
        out_shape=(
            jax.ShapeDtypeStruct(sky.shape, BF16),
            jax.ShapeDtypeStruct(conv_f.shape, F32),
            jax.ShapeDtypeStruct(conv_c.shape, F32),
            jax.ShapeDtypeStruct(head.shape, F32),
        ),
        in_specs=[vmem] * 9,
        out_specs=(vmem,) * 4,
        scratch_shapes=[
            pltpu.VMEM((ORDER, rows, LANES), F32),
            pltpu.VMEM((rows, LANES), jnp.int32),
            pltpu.VMEM((rows, LANES), F32),
            pltpu.VMEM((8, rows, LANES), jnp.int32),
            pltpu.VMEM((8, rows, LANES), F32),
            pltpu.VMEM((rows, LANES), F32),
            pltpu.VMEM((ORDER * 8, pixels), BF16),
            pltpu.VMEM((pixels, pixels // 16), BF16),
            pltpu.VMEM((held, 24, LANES), F32),
            pltpu.VMEM((held, 32, LANES), F32),
            pltpu.VMEM((held // 2, 4 * LANES, 2 * LANES), BF16),
            pltpu.VMEM((200, LANES), F32),
            pltpu.VMEM((200, LANES), F32),
            pltpu.VMEM((16, LANES), F32),
            pltpu.VMEM((16, LANES), F32),
            pltpu.VMEM((held, 16, LANES), F32),
            pltpu.VMEM((8, LANES), F32),
            dma((6,)), dma((6,)),
            dma((held,)), dma((held,)),
            dma((held,)), dma((held,)),
            dma((2,)), dma((2,)),
            dma((held,)), dma((held,)),
        ],
        compiler_params=pltpu.CompilerParams(
            collective_id=0, has_side_effects=True, vmem_limit_bytes=40 * 1024 * 1024
        ),
        name="unet",
    )(*args)
    if not full:
        pred, grad_fine, grad_coarse, grad_head = result
        grads = lax.psum((grad_fine, grad_coarse, grad_head), ("patch", "sub", "rep"))
        result = (pred, *grads)
    return tuple(result)


def solution(mesh):
    pixel = P(None, ("patch", "sub"))
    maps = P(("parts", "rep"), None, ("patch", "sub"))
    ring = (mesh.shape["patch"], mesh.shape["sub"])
    return jax.shard_map(
        partial(on_device, ring, mesh.shape["rep"]),
        mesh=mesh,
        in_specs=(maps, pixel, pixel, pixel, pixel, P(), P(), P(), maps),
        out_specs=(maps, P("parts", None), P("parts", None), P("parts", None)),
        check_vma=False,
    )
```

time: 627 us -> 38.4 us (0.06); the launches traced: 619 us -> 37.9 us
  local copies, waits for them, and re-layouts: 354 us -> 8.75 us
  waiting for transfers between devices: 68.5 us -> 0 us
  other arithmetic: 66.6 us -> 0 us
  blocking collectives: 58.1 us -> 0 us
  starting transfers between devices: 52.2 us -> 0 us
  Pallas kernels: 0 us -> 28.5 us
  between operations: 16.4 us -> 0.68 us
    gather x160 -> x0, local copies, waits for them, and re-layouts: 336 us -> none  [the longest x140 300 us: slot_sum(): nearby = nearby + weight[column] * values[:, index[column]]]
    psum x1 -> x0, blocking collectives: 58.1 us -> none  [on_device(): grad_one = lax.psum(grad_one, ('patch', 'sub', 'rep'))]
    scatter-add x40 -> x0, other arithmetic: 53.4 us -> none  [coarse_adjoint(): spread = spread.at[:, index[column]].add(weight[column] * field)]
    ppermute x30 -> x0, starting transfers between devices: 52.1 us -> none  [the longest x10 24.2 us: shifted(): lax.ppermute(x, axis, [(i, (i + by) % length) for i in range(length)])]
    ppermute x30 -> x0, waiting for transfers between devices: 44.1 us -> none  [the longest x10 27.7 us: extended_2(): lax.ppermute(lax.slice_in_dim(block, block.shape[dim] - width, None, axis...]
    pallas_call x0 -> x1, Pallas kernels: none -> 28.5 us  [on_device(): pl.pallas_call(partial(kernel, ring, reps, scale), out_shape=(jax.ShapeDt...]
    psum x1 -> x0, waiting for transfers between devices: 24.3 us -> none  [on_device(): grad_two = lax.psum(grad_two, ('patch', 'sub', 'rep'))]
  transfers between devices with their start and end apart: 31 -> 0, of which waited for: 24 -> 0; matrix products, arithmetic and copies ran while one was open for 3% -> 0% of each run, Pallas kernels for 0% -> 0%
where the time goes in v1:
time: 38.4 us; the launch traced here: 37.9 us
  Pallas kernels  28.5 us (74%)
  local copies, waits for them, and re-layouts  8.75 us (23%)
  between operations  0.68 us (2%)
    pallas_call x1, Pallas kernels, on_device(): pl.pallas_call(partial(kernel, ring, reps, scale), out_shape=(jax.ShapeDt...  28.5 us
    unnamed x18, local copies, waits for them, and re-layouts  7.4 us
    pallas_call x2, local copies, waits for them, and re-layouts, on_device(): pl.pallas_call(partial(kernel, ring, reps, scale), out_shape=(jax.ShapeDt...  1.35 us

profile of v1, /device:TPU:0, one launch (start us, length us, event | category | flops | bytes accessed | tf_op | source)
XLA Modules:
  0.0 37.9 jit_solution(16314477757393614332)
XLA Ops:
  0.6 0.0 copy-start
  0.6 0.8 %copy.13.conv_f = bf16[48,32]{1,0:T(8,128)(2,1)S(1)} copy(bf16[48,32]{0,1:T(8,128)(2,1)} %param.14) | data formatting | bytes 6144 | tf_op args[5]
  1.5 0.8 %copy.14.head = bf16[160,8]{1,0:T(8,128)(2,1)S(1)} copy(bf16[160,8]{0,1:T(8,128)(2,1)} %param.16) | data formatting | bytes 5120 | tf_op args[7]
  2.3 0.0 copy-done
  2.3 0.0 copy-start.1
  2.3 0.8 %copy-done.1 = f32[8,2048]{1,0:T(8,128)S(1)} copy-done((f32[8,2048]{1,0:T(8,128)S(1)}, f32[8,2048]{1,0:T(8,128)}, u32[]{:S(2)}) %copy-start.1) | copy-done | bytes 65560
  3.1 0.0 copy-start.2
  3.1 0.8 %copy-done.2 = bf16[192,128]{1,0:T(8,128)(2,1)S(1)} copy-done((bf16[192,128]{1,0:T(8,128)(2,1)S(1)}, bf16[192,128]{1,0:T(8,128)(2,1)}, u32[]{:S(2)}) %copy-start.2) | copy-done | bytes 49176
  3.9 0.0 copy-start.3
  3.9 0.8 %copy-done.3 = bf16[1,8,2048]{2,1,0:T(8,128)(2,1)S(1)} copy-done((bf16[1,8,2048]{2,1,0:T(8,128)(2,1)S(1)}, bf16[1,8,2048]{2,1,0:T(8,128)(2,1)}, u32[]{:S(2)}) %copy-start.3) | copy-done | bytes 32792
  4.7 0.0 copy-start.4
  4.7 0.8 %copy-done.4 = bf16[1,8,2048]{2,1,0:T(8,128)(2,1)S(1)} copy-done((bf16[1,8,2048]{2,1,0:T(8,128)(2,1)S(1)}, bf16[1,8,2048]{2,1,0:T(8,128)(2,1)}, u32[]{:S(2)}) %copy-start.4) | copy-done | bytes 32792
  5.4 0.0 copy-start.5
  5.4 0.7 %copy-done.5 = s32[8,128]{1,0:T(8,128)S(1)} copy-done((s32[8,128]{1,0:T(8,128)S(1)}, s32[8,128]{1,0:T(8,128)}, u32[]{:S(2)}) %copy-start.5) | copy-done | bytes 4120
  6.1 0.0 copy-start.6
  6.1 0.7 %copy-done.6 = f32[8,128]{1,0:T(8,128)S(1)} copy-done((f32[8,128]{1,0:T(8,128)S(1)}, f32[8,128]{1,0:T(8,128)}, u32[]{:S(2)}) %copy-start.6) | copy-done | bytes 4120
  6.8 28.5 %unet.1 = (bf16[1,8,2048]{2,1,0:T(8,128)(2,1)S(1)}, f32[48,32]{1,0:T(8,128)S(1)}, f32[192,128]{1,0:T(8,128)S(1)}, f32[160,8]{1,0:T(8,128)S(1)}) custom-call(bf16[1,8,2048]{2,1,0:T(8,128)(2,1)S(1)} %copy-done.3, s32[8,2048]{1,0:T(8,128)S(1)} %copy-done, f32[8,2048]{1,0:T(8,128)S(1)} %copy-done.1, s32[8,128]{1,0:T(8,128)S(1)} %copy-done.5, ...), custom_call_target="tpu_custom_call" | custom-call | tf_op jit(solution)/shard_map/unet/pallas_call | solution.py:312
  35.3 0.7 %copy.16 = f32[160,8]{0,1:T(8,128)} copy(f32[160,8]{1,0:T(8,128)S(1)} %get-tuple-element.7) | data formatting | bytes 10240 | tf_op jit(solution)/shard_map/unet/pallas_call | solution.py:312
  36.0 0.7 %copy.15 = f32[48,32]{0,1:T(8,128)} copy(f32[48,32]{1,0:T(8,128)S(1)} %get-tuple-element.5) | data formatting | bytes 12288 | tf_op jit(solution)/shard_map/unet/pallas_call | solution.py:312
  36.7 0.6 %copy.19 = bf16[1,8,2048]{2,1,0:T(8,128)(2,1)} copy(bf16[1,8,2048]{2,1,0:T(8,128)(2,1)S(1)} %get-tuple-element.12) | data formatting | bytes 65536
  37.3 0.6 %copy.20 = f32[192,128]{1,0:T(8,128)} copy(f32[192,128]{1,0:T(8,128)S(1)} %get-tuple-element.14) | data formatting | bytes 196608
Async XLA Ops:
  0.6 1.6 %copy-start = (s32[8,2048]{1,0:T(8,128)S(1)}, s32[8,2048]{1,0:T(8,128)}, u32[]{:S(2)}) copy-start(s32[8,2048]{1,0:T(8,128)} %nbf.1) | copy-start | bytes 196612
  2.3 0.8 %copy-start.1 = (f32[8,2048]{1,0:T(8,128)S(1)}, f32[8,2048]{1,0:T(8,128)}, u32[]{:S(2)}) copy-start(f32[8,2048]{1,0:T(8,128)} %wf.1) | copy-start | bytes 196612
  3.1 0.8 %copy-start.2 = (bf16[192,128]{1,0:T(8,128)(2,1)S(1)}, bf16[192,128]{1,0:T(8,128)(2,1)}, u32[]{:S(2)}) copy-start(bf16[192,128]{1,0:T(8,128)(2,1)} %conv_c.1) | copy-start | bytes 147460
  3.9 0.8 %copy-start.3 = (bf16[1,8,2048]{2,1,0:T(8,128)(2,1)S(1)}, bf16[1,8,2048]{2,1,0:T(8,128)(2,1)}, u32[]{:S(2)}) copy-start(bf16[1,8,2048]{2,1,0:T(8,128)(2,1)} %sky.1) | copy-start | bytes 98308
  4.7 0.8 %copy-start.4 = (bf16[1,8,2048]{2,1,0:T(8,128)(2,1)S(1)}, bf16[1,8,2048]{2,1,0:T(8,128)(2,1)}, u32[]{:S(2)}) copy-start(bf16[1,8,2048]{2,1,0:T(8,128)(2,1)} %cot.1) | copy-start | bytes 98308
  5.4 0.7 %copy-start.5 = (s32[8,128]{1,0:T(8,128)S(1)}, s32[8,128]{1,0:T(8,128)}, u32[]{:S(2)}) copy-start(s32[8,128]{1,0:T(8,128)} %nbc.1) | copy-start | bytes 12292
  6.1 0.7 %copy-start.6 = (f32[8,128]{1,0:T(8,128)S(1)}, f32[8,128]{1,0:T(8,128)}, u32[]{:S(2)}) copy-start(f32[8,128]{1,0:T(8,128)} %wc.1) | copy-start | bytes 12292

commit v2 on v1

--- a/solution.py
+++ b/solution.py
@@ -11,6 +11,7 @@
 ORDER = 6
 LANES = 128
 REACH = ORDER - 1
+VMEM_BYTES = 64 * 1024 * 1024
 MESH = pl.DeviceIdType.MESH
 F32 = jnp.float32
 BF16 = jnp.bfloat16
@@ -39,11 +40,22 @@
 
 
 def kernel(
-    ring, reps, scale, sky, nbf, wf, nbc, wc, conv_f, conv_c, head, cot,
-    pred, out_fine, out_coarse, out_head,
+    ring, reps, scale, *refs
+):
+    hbm = refs[:9]
+    results = refs[9:13]
+    local = refs[13:22]
+    sky, nbf, wf, nbc, wc, conv_f, conv_c, head, cot = local
+    (
     field, nb, wt, idx8, w8, deg, stack, pool, cg, pg, mat, gc, gc_in, pack, pack_in, total, all_in,
     halo_send, halo_recv, cg_send, cg_recv, pg_send, pg_recv, rep_send, rep_recv, all_send, all_recv,
-):
+        load_sem, pred, out_fine, out_coarse, out_head, store_sem,
+    ) = refs[22:]
+    loads = [
+        pltpu.make_async_copy(hbm[n], local[n], load_sem.at[n]) for n in range(9)
+    ]
+    for n in (0, 1, 2, 8, 3, 4, 5, 7, 6):
+        loads[n].start()
     patches, subs = ring
     count = patches * subs
     full, held, offsets, peers = window_of(count)
@@ -63,6 +75,8 @@
     if full:
         pl.semaphore_signal(barrier, inc=1, device_id=partner, device_id_type=MESH)
 
+    for n in range(3):
+        loads[n].wait()
     for b in range(blocks):
         rows = slice((first + b) * 8, (first + b + 1) * 8)
         lanes = slice(b * LANES, (b + 1) * LANES)
@@ -93,6 +107,8 @@
     pixel = lax.broadcasted_iota(jnp.int32, pool.shape, 0)
     coarse = lax.broadcasted_iota(jnp.int32, pool.shape, 1)
     pool[...] = jnp.where((pixel >> 4) == coarse, 1.0, 0.0).astype(BF16)
+    for n in (8, 3, 4):
+        loads[n].wait()
     signal = (cot[0].astype(F32) * scale).astype(BF16)
     pooled_signal = dot(signal, pool[...])
     cg[0, 0:8, :] = nbc[...].astype(F32)
@@ -155,7 +171,9 @@
         tile = field[:, slice((first + b) * 8, (first + b + 1) * 8), :]
         stack[:, slice(b * LANES, (b + 1) * LANES)] = tile.reshape(ORDER * 8, LANES).astype(BF16)
 
-    fine_pre = dot(conv_f[...], stack[...], ((0,), (0,)))
+    for n in (5, 6, 7):
+        loads[n].wait()
+    fine_pre = dot(conv_f[...], stack[...])
     fine_gate = gate(fine_pre)
     hidden = (fine_pre * fine_gate).astype(BF16)
     pg[0] = dot(hidden, pool[...]) * 0.0625
@@ -167,10 +185,10 @@
 
     grad_top = dot(signal, hidden, ((1,), (1,)))
     fine_slope = fine_gate * (1.0 + fine_pre * (1.0 - fine_gate))
-    head_fine = head[0:32, :]
-    head_coarse = head[32:160, :]
-    direct = dot(head_fine, signal)
-    result_fine = dot(head_fine, hidden, ((0,), (0,)))
+    head_fine = head[:, 0:32]
+    head_coarse = head[:, 32:160]
+    direct = dot(head_fine, signal, ((0,), (0,)))
+    result_fine = dot(head_fine, hidden)
 
     for copy in gathers:
         copy.wait()
@@ -195,7 +213,7 @@
     degree = jnp.concatenate(degrees, axis=1)
     signals = jnp.concatenate([cg[t, 16:24, :] for t in range(held)], axis=1)
     sig_high, sig_low = split2(signals)
-    coarse_back = dot(head_coarse, sig_high) + dot(head_coarse, sig_low)
+    coarse_back = dot(head_coarse, sig_high, ((0,), (0,))) + dot(head_coarse, sig_low, ((0,), (0,)))
 
     for copy in pooled_gathers:
         copy.wait()
@@ -251,11 +269,10 @@
     grad_high, grad_low_part = split2(pooled_grad)
     raised = dot(jnp.concatenate([grad_high, grad_low_part], axis=0), pool[...], pool_t)
     fine_delta = ((direct + raised[:32] + raised[32:]) * fine_slope).astype(BF16)
-    grad_fine = dot(stack[...], fine_delta, pool_t)
-
-    pack[:, 0:32] = grad_fine[0:16]
-    pack[:, 32:64] = grad_fine[16:32]
-    pack[:, 64:96] = grad_fine[32:48]
+    grad_fine = dot(fine_delta, stack[...], pool_t)
+
+    pack[:, 0:48] = grad_fine[0:16]
+    pack[:, 48:96] = grad_fine[16:32]
     pack[0:8, 96:128] = grad_top
     pack[8:16, 96:128] = jnp.zeros((8, 32), F32)
     if full:
@@ -276,14 +293,21 @@
                 push(total.at[0], total.at[back], all_send.at[p], all_recv.at[back], at(offsets[p])))
         pair_coarse = push(gc, gc_in, rep_send.at[1], rep_recv.at[1], partner)
 
-    upward = dot(head_coarse, coarse_hidden[:, :LANES], ((0,), (0,)))
+    upward = dot(head_coarse, coarse_hidden[:, :LANES])
     up_high, up_low = split2(upward)
     result = result_fine + dot(up_high, pool[...], pool_t) + dot(up_low, pool[...], pool_t)
     pred[0] = result.astype(BF16)
+    stores = [
+        pltpu.make_async_copy(src, results[n], store_sem.at[n])
+        for n, src in enumerate((pred, out_fine, out_coarse, out_head))
+    ]
+    stores[0].start()
 
     if full:
         pair_coarse.wait()
         sums = gc[...] + gc_in[...]
+        out_coarse[...] = sums[0:192]
+        stores[2].start()
         for copy in spreads:
             copy.wait()
         whole = total[0]
@@ -292,15 +316,28 @@
     else:
         sums = gc[...]
         whole = pack[...]
-    out_coarse[...] = sums[0:192]
-    out_fine[0:16, :] = whole[:, 0:32]
-    out_fine[16:32, :] = whole[:, 32:64]
-    out_fine[32:48, :] = whole[:, 64:96]
-    out_head[0:32, :] = jnp.transpose(whole[0:8, 96:128])
-    out_head[32:160, :] = jnp.transpose(sums[192:200])
+        out_coarse[...] = sums[0:192]
+        stores[2].start()
+    out_fine[0:16, :] = whole[:, 0:48]
+    out_fine[16:32, :] = whole[:, 48:96]
+    out_head[:, 0:32] = whole[0:8, 96:128]
+    out_head[:, 32:160] = sums[192:200]
+    stores[1].start()
+    stores[3].start()
+    for copy in stores:
+        copy.wait()
+
+
+def write_out(*refs):
+    copies = [pltpu.make_async_copy(refs[n], refs[4 + n], refs[8].at[n]) for n in range(4)]
+    for copy in copies:
+        copy.start()
+    for copy in copies:
+        copy.wait()
 
 
 def on_device(ring, reps, *args):
+    args = (*args[:5], args[5].T, args[6], args[7].T, args[8])
     sky, conv_f, conv_c, head = args[0], args[5], args[6], args[7]
     pixels = sky.shape[2]
     count = ring[0] * ring[1]
@@ -308,18 +345,20 @@
     rows = (pixels // LANES + 2 * REACH) * 8
     scale = 1.0 / math.sqrt(pixels * count * sky.shape[0] * reps)
     dma = pltpu.SemaphoreType.DMA
-    vmem = pl.BlockSpec(memory_space=pltpu.VMEM)
+    hbm = pl.BlockSpec(memory_space=pltpu.HBM)
+    shapes = (
+        jax.ShapeDtypeStruct(sky.shape, BF16),
+        jax.ShapeDtypeStruct(conv_f.shape, F32),
+        jax.ShapeDtypeStruct(conv_c.shape, F32),
+        jax.ShapeDtypeStruct(head.shape, F32),
+    )
     result = pl.pallas_call(
         partial(kernel, ring, reps, scale),
-        out_shape=(
-            jax.ShapeDtypeStruct(sky.shape, BF16),
-            jax.ShapeDtypeStruct(conv_f.shape, F32),
-            jax.ShapeDtypeStruct(conv_c.shape, F32),
-            jax.ShapeDtypeStruct(head.shape, F32),
-        ),
-        in_specs=[vmem] * 9,
-        out_specs=(vmem,) * 4,
+        out_shape=shapes,
+        in_specs=[hbm] * 9,
+        out_specs=(hbm,) * 4,
         scratch_shapes=[
+            *[pltpu.VMEM(a.shape, a.dtype) for a in args],
             pltpu.VMEM((ORDER, rows, LANES), F32),
             pltpu.VMEM((rows, LANES), jnp.int32),
             pltpu.VMEM((rows, LANES), F32),
@@ -342,12 +381,27 @@
             dma((held,)), dma((held,)),
             dma((2,)), dma((2,)),
             dma((held,)), dma((held,)),
+            dma((9,)),
+            *[pltpu.VMEM(r.shape, r.dtype) for r in shapes],
+            dma((4,)),
         ],
         compiler_params=pltpu.CompilerParams(
-            collective_id=0, has_side_effects=True, vmem_limit_bytes=40 * 1024 * 1024
+            collective_id=0, has_side_effects=True, vmem_limit_bytes=VMEM_BYTES
         ),
         name="unet",
     )(*args)
+    if full:
+        result = pl.pallas_call(
+            write_out,
+            out_shape=shapes,
+            in_specs=[hbm] * 4,
+            out_specs=(hbm,) * 4,
+            scratch_shapes=[dma((4,))],
+            compiler_params=pltpu.CompilerParams(vmem_limit_bytes=VMEM_BYTES),
+            name="write_out",
+        )(*result)
+    pred, grad_fine, grad_coarse, grad_head = result
+    result = (pred, grad_fine.T, grad_coarse, grad_head.T)
     if not full:
         pred, grad_fine, grad_coarse, grad_head = result
         grads = lax.psum((grad_fine, grad_coarse, grad_head), ("patch", "sub", "rep"))

time: 38.4 us -> 36 us (0.938)
  local copies, waits for them, and re-layouts: 8.75 us -> 0 us
  Pallas kernels: 28.5 us -> 35.2 us
    unnamed x18 -> x0, local copies, waits for them, and re-layouts: 7.4 us -> none
    pallas_call x1 -> x2, Pallas kernels: 28.5 us -> 35.2 us  [the longest x1 29.3 us: on_device(): pl.pallas_call(partial(kernel, ring, reps, scale), out_shape=shapes, in_s...]
    pallas_call x2 -> x0, local copies, waits for them, and re-layouts: 1.35 us -> none  [on_device(): pl.pallas_call(partial(kernel, ring, reps, scale), out_shape=(jax.ShapeDt...]
where the time goes in v2:
time: 36 us; the launch traced here: 35.8 us
  Pallas kernels  35.2 us (98%)
  between operations  0.64 us (2%)
    pallas_call x1, Pallas kernels, on_device(): pl.pallas_call(partial(kernel, ring, reps, scale), out_shape=shapes, in_s...  29.3 us
    pallas_call x1, Pallas kernels, on_device(): pl.pallas_call(write_out, out_shape=shapes, in_specs=[hbm] * 4, out_specs...  5.85 us

profile of v2, /device:TPU:0, one launch (start us, length us, event | category | flops | bytes accessed | tf_op | source)
XLA Modules:
  0.0 35.8 jit_solution(5394801061741089912)
XLA Ops:
  0.6 29.3 %unet.1 = (bf16[1,8,2048]{2,1,0:T(8,128)(2,1)}, f32[32,48]{1,0:T(8,128)}, f32[192,128]{1,0:T(8,128)}, f32[8,160]{1,0:T(8,128)}) custom-call(bf16[1,8,2048]{2,1,0:T(8,128)(2,1)} %refs_0_.1, s32[8,2048]{1,0:T(8,128)} %refs_1_.1, f32[8,2048]{1,0:T(8,128)} %refs_2_.1, s32[8,128]{1,0:T(8,128)} %refs_3_.1, f32[8,128]{1,0:T(8,128)} %refs_4_.1, ...), custom_call_target="tpu_custom_call" | custom-call | tf_op jit(solution)/shard_map/unet/pallas_call | solution.py:355
  29.9 5.9 %write_out.1 = (bf16[1,8,2048]{2,1,0:T(8,128)(2,1)}, f32[32,48]{1,0:T(8,128)}, f32[192,128]{1,0:T(8,128)}, f32[8,160]{1,0:T(8,128)}) custom-call(bf16[1,8,2048]{2,1,0:T(8,128)(2,1)} %get-tuple-element.12.refs_0_, f32[32,48]{1,0:T(8,128)} %get-tuple-element.13.refs_1_, f32[192,128]{1,0:T(8,128)} %get-tuple-element.14.refs_2_, f32[8,160]{1,0:T(8,128)} %get-tuple-element.15.refs_3_), custom_call_target="tpu_custom_call" | custom-call | tf_op jit(solution)/shard_map/write_out/pallas_call | solution.py:394

commit v3 on v2

--- a/solution.py
+++ b/solution.py
@@ -47,7 +47,7 @@
     local = refs[13:22]
     sky, nbf, wf, nbc, wc, conv_f, conv_c, head, cot = local
     (
-    field, nb, wt, idx8, w8, deg, stack, pool, cg, pg, mat, gc, gc_in, pack, pack_in, total, all_in,
+    field, nb, wt, idx8, w8, deg, stack, pool, cg, pg, mat, gc, gc_in, pack, pack_in, total, halo_out, halo_in,
     halo_send, halo_recv, cg_send, cg_recv, pg_send, pg_recv, rep_send, rep_recv, all_send, all_recv,
         load_sem, pred, out_fine, out_coarse, out_head, store_sem,
     ) = refs[22:]
@@ -93,16 +93,18 @@
         copy.start()
         return copy
 
-    halos = []
-    for n, (ref, width) in enumerate(((field.at[0], REACH), (nb, REACH - 1), (wt, REACH - 1))):
-        size = width * 8
-        skip = (REACH - width) * 8
-        halos.append(push(
-            ref.at[pl.ds(last * 8 - size, size)], ref.at[pl.ds(skip, size)],
-            halo_send.at[2 * n], halo_recv.at[2 * n], at(1)))
-        halos.append(push(
-            ref.at[pl.ds(first * 8, size)], ref.at[pl.ds(last * 8, size)],
-            halo_send.at[2 * n + 1], halo_recv.at[2 * n + 1], at(-1)))
+    def ends(b0):
+        inner = slice((b0 if b0 == first else b0 + 1) * 8, (b0 + REACH - (b0 == first)) * 8)
+        return jnp.concatenate([
+            field[0, slice(b0 * 8, (b0 + REACH) * 8), :], jnp.zeros((8, LANES), F32),
+            nb[inner, :].astype(F32), wt[inner, :]], axis=0).astype(BF16)
+
+    halo_out[0] = ends(last - REACH)
+    halo_out[1] = ends(first)
+    halos = [
+        push(halo_out.at[n], halo_in.at[n], halo_send.at[n], halo_recv.at[n], at(1 - 2 * n))
+        for n in range(2)
+    ]
 
     pixel = lax.broadcasted_iota(jnp.int32, pool.shape, 0)
     coarse = lax.broadcasted_iota(jnp.int32, pool.shape, 1)
@@ -111,13 +113,9 @@
         loads[n].wait()
     signal = (cot[0].astype(F32) * scale).astype(BF16)
     pooled_signal = dot(signal, pool[...])
-    cg[0, 0:8, :] = nbc[...].astype(F32)
-    cg[0, 8:16, :] = wc[...] * 0.125
-    cg[0, 16:24, :] = pooled_signal
-    gathers = []
-    for p in peers:
-        back = (held - p) % held
-        gathers.append(push(cg.at[0], cg.at[back], cg_send.at[p], cg_recv.at[back], at(offsets[p])))
+    cg[0] = jnp.concatenate([
+        nbc[...].astype(F32), wc[...] * 0.125, pooled_signal,
+        pooled_signal - pooled_signal.astype(BF16).astype(F32)], axis=0).astype(BF16)
 
     def spread_slots(b0, b1):
         shape = (b1 - b0, 8, LANES)
@@ -162,6 +160,16 @@
         level(k, first + k, last - k)
     for copy in halos:
         copy.wait()
+    gathers = []
+    for p in peers:
+        back = (held - p) % held
+        gathers.append(push(cg.at[0], cg.at[back], cg_send.at[p], cg_recv.at[back], at(offsets[p])))
+    for n, (b0, skip) in enumerate(((0, 1), (last, 0))):
+        got = halo_in[n].astype(F32)
+        inner = slice((b0 + skip) * 8, (b0 + skip + REACH - 1) * 8)
+        field[0, slice(b0 * 8, (b0 + REACH) * 8), :] = got[: REACH * 8]
+        nb[inner, :] = got[48:80].astype(jnp.int32)
+        wt[inner, :] = got[80:112]
     spread_slots(1, first)
     spread_slots(last, last + REACH - 1)
     for k in range(1, ORDER):
@@ -176,7 +184,7 @@
     fine_pre = dot(conv_f[...], stack[...])
     fine_gate = gate(fine_pre)
     hidden = (fine_pre * fine_gate).astype(BF16)
-    pg[0] = dot(hidden, pool[...]) * 0.0625
+    pg[0] = (dot(hidden, pool[...]) * 0.0625).astype(BF16)
     pooled_gathers = []
     for p in peers:
         back = (held - p) % held
@@ -196,10 +204,11 @@
         cg[held // 2] = cg[0]
     source = lax.broadcasted_iota(jnp.int32, (3 * LANES, LANES), 0)
     lane = lax.broadcasted_iota(jnp.int32, (8, LANES), 1)
-    degrees = []
+    degrees, signals = [], []
     for t in range(held):
-        offs = cg[t, 0:8, :].astype(jnp.int32) + lane + LANES
-        weight = cg[t, 8:16, :]
+        tables = cg[t].astype(F32)
+        offs = tables[0:8].astype(jnp.int32) + lane + LANES
+        weight = tables[8:16]
         block = None
         for j in range(8):
             term = jnp.where(offs[j : j + 1, :] == source, weight[j : j + 1, :], 0.0)
@@ -210,9 +219,10 @@
         empty = 3 * LANES if side == 0 else 0
         mat[u, slice(empty, empty + LANES), cols] = jnp.zeros((LANES, LANES), BF16)
         degrees.append(jnp.sum(weight, axis=0, keepdims=True) - 1.0)
+        signals.append(tables[16:32])
     degree = jnp.concatenate(degrees, axis=1)
-    signals = jnp.concatenate([cg[t, 16:24, :] for t in range(held)], axis=1)
-    sig_high, sig_low = split2(signals)
+    signals = jnp.concatenate(signals, axis=1)
+    sig_high, sig_low = signals[0:8].astype(BF16), signals[8:16].astype(BF16)
     coarse_back = dot(head_coarse, sig_high, ((0,), (0,))) + dot(head_coarse, sig_low, ((0,), (0,)))
 
     for copy in pooled_gathers:
@@ -247,7 +257,7 @@
                 sums[s] = piece if sums[s] is None else sums[s] + piece
         return degree * x - jnp.concatenate(sums, axis=1)
 
-    poly = [jnp.concatenate([pg[t] for t in range(held)], axis=1)]
+    poly = [jnp.concatenate([pg[t] for t in range(held)], axis=1).astype(F32)]
     poly.append(forward(poly[0]))
     for k in range(2, ORDER):
         poly.append(2.0 * forward(poly[-1]) - poly[-2])
@@ -284,14 +294,14 @@
         sig_low[:, span], coarse_hidden[:, span], pool_t)
 
     if full:
+        pair_coarse = push(gc, gc_in, rep_send.at[1], rep_recv.at[1], partner)
         pair.wait()
-        total[0] = pack[...] + pack_in[...]
+        total[0] = (pack[...] + pack_in[...]).astype(BF16)
         spreads = []
         for p in peers:
             back = (held - p) % held
             spreads.append(
                 push(total.at[0], total.at[back], all_send.at[p], all_recv.at[back], at(offsets[p])))
-        pair_coarse = push(gc, gc_in, rep_send.at[1], rep_recv.at[1], partner)
 
     upward = dot(head_coarse, coarse_hidden[:, :LANES])
     up_high, up_low = split2(upward)
@@ -310,9 +320,9 @@
         stores[2].start()
         for copy in spreads:
             copy.wait()
-        whole = total[0]
+        whole = total[0].astype(F32)
         for t in range(1, held):
-            whole = whole + total[t]
+            whole = whole + total[t].astype(F32)
     else:
         sums = gc[...]
         whole = pack[...]
@@ -329,10 +339,15 @@
 
 
 def write_out(*refs):
-    copies = [pltpu.make_async_copy(refs[n], refs[4 + n], refs[8].at[n]) for n in range(4)]
-    for copy in copies:
+    held, sems = refs[8:12], refs[12]
+    loads = [pltpu.make_async_copy(refs[n], held[n], sems.at[n]) for n in range(4)]
+    stores = [pltpu.make_async_copy(held[n], refs[4 + n], sems.at[4 + n]) for n in range(4)]
+    for copy in loads:
         copy.start()
-    for copy in copies:
+    for load, store in zip(loads, stores):
+        load.wait()
+        store.start()
+    for copy in stores:
         copy.wait()
 
 
@@ -367,16 +382,17 @@
             pltpu.VMEM((rows, LANES), F32),
             pltpu.VMEM((ORDER * 8, pixels), BF16),
             pltpu.VMEM((pixels, pixels // 16), BF16),
-            pltpu.VMEM((held, 24, LANES), F32),
-            pltpu.VMEM((held, 32, LANES), F32),
+            pltpu.VMEM((held, 32, LANES), BF16),
+            pltpu.VMEM((held, 32, LANES), BF16),
             pltpu.VMEM((held // 2, 4 * LANES, 2 * LANES), BF16),
             pltpu.VMEM((200, LANES), F32),
             pltpu.VMEM((200, LANES), F32),
             pltpu.VMEM((16, LANES), F32),
             pltpu.VMEM((16, LANES), F32),
-            pltpu.VMEM((held, 16, LANES), F32),
-            pltpu.VMEM((8, LANES), F32),
-            dma((6,)), dma((6,)),
+            pltpu.VMEM((held, 16, LANES), BF16),
+            pltpu.VMEM((2, 112, LANES), BF16),
+            pltpu.VMEM((2, 112, LANES), BF16),
+            dma((2,)), dma((2,)),
             dma((held,)), dma((held,)),
             dma((held,)), dma((held,)),
             dma((2,)), dma((2,)),
@@ -396,7 +412,7 @@
             out_shape=shapes,
             in_specs=[hbm] * 4,
             out_specs=(hbm,) * 4,
-            scratch_shapes=[dma((4,))],
+            scratch_shapes=[*[pltpu.VMEM(r.shape, r.dtype) for r in shapes], dma((8,))],
             compiler_params=pltpu.CompilerParams(vmem_limit_bytes=VMEM_BYTES),
             name="write_out",
         )(*result)

time: 36 us -> 30.1 us (0.84)
  Pallas kernels: 35.2 us -> 29.2 us
    pallas_call x1, Pallas kernels: 5.85 us -> 1.64 us  [on_device(): pl.pallas_call(write_out, out_shape=shapes, in_specs=[hbm] * 4, out_specs...]
    pallas_call x1, Pallas kernels: 29.3 us -> 27.6 us  [on_device(): pl.pallas_call(partial(kernel, ring, reps, scale), out_shape=shapes, in_s...]
where the time goes in v3:
time: 30.1 us; the launch traced here: 29.9 us
  Pallas kernels  29.2 us (97%)
  between operations  0.64 us (2%)
    pallas_call x1, Pallas kernels, on_device(): pl.pallas_call(partial(kernel, ring, reps, scale), out_shape=shapes, in_s...  27.6 us
    pallas_call x1, Pallas kernels, on_device(): pl.pallas_call(write_out, out_shape=shapes, in_specs=[hbm] * 4, out_specs...  1.64 us

profile of v3, /device:TPU:0, one launch (start us, length us, event | category | flops | bytes accessed | tf_op | source)
XLA Modules:
  0.0 29.9 jit_solution(9236312025803013834)
XLA Ops:
  0.6 27.6 %unet.1 = (bf16[1,8,2048]{2,1,0:T(8,128)(2,1)}, f32[32,48]{1,0:T(8,128)}, f32[192,128]{1,0:T(8,128)}, f32[8,160]{1,0:T(8,128)}) custom-call(bf16[1,8,2048]{2,1,0:T(8,128)(2,1)} %refs_0_.1, s32[8,2048]{1,0:T(8,128)} %refs_1_.1, f32[8,2048]{1,0:T(8,128)} %refs_2_.1, s32[8,128]{1,0:T(8,128)} %refs_3_.1, f32[8,128]{1,0:T(8,128)} %refs_4_.1, ...), custom_call_target="tpu_custom_call" | custom-call | tf_op jit(solution)/shard_map/unet/pallas_call | solution.py:370
  28.2 1.6 %write_out.1 = (bf16[1,8,2048]{2,1,0:T(8,128)(2,1)}, f32[32,48]{1,0:T(8,128)}, f32[192,128]{1,0:T(8,128)}, f32[8,160]{1,0:T(8,128)}) custom-call(bf16[1,8,2048]{2,1,0:T(8,128)(2,1)} %get-tuple-element.12.refs_0_, f32[32,48]{1,0:T(8,128)} %get-tuple-element.13.refs_1_, f32[192,128]{1,0:T(8,128)} %get-tuple-element.14.refs_2_, f32[8,160]{1,0:T(8,128)} %get-tuple-element.15.refs_3_), custom_call_target="tpu_custom_call" | custom-call | tf_op jit(solution)/shard_map/write_out/pallas_call | solution.py:410

commit v4 on v3

--- a/solution.py
+++ b/solution.py
@@ -117,6 +117,11 @@
         nbc[...].astype(F32), wc[...] * 0.125, pooled_signal,
         pooled_signal - pooled_signal.astype(BF16).astype(F32)], axis=0).astype(BF16)
 
+    gathers = []
+    for p in peers:
+        back = (held - p) % held
+        gathers.append(push(cg.at[0], cg.at[back], cg_send.at[p], cg_recv.at[back], at(offsets[p])))
+
     def spread_slots(b0, b1):
         shape = (b1 - b0, 8, LANES)
         rows = slice(b0 * 8, b1 * 8)
@@ -160,10 +165,6 @@
         level(k, first + k, last - k)
     for copy in halos:
         copy.wait()
-    gathers = []
-    for p in peers:
-        back = (held - p) % held
-        gathers.append(push(cg.at[0], cg.at[back], cg_send.at[p], cg_recv.at[back], at(offsets[p])))
     for n, (b0, skip) in enumerate(((0, 1), (last, 0))):
         got = halo_in[n].astype(F32)
         inner = slice((b0 + skip) * 8, (b0 + skip + REACH - 1) * 8)
@@ -233,29 +234,26 @@
     wide = held * LANES
 
     def forward(x):
-        rows = x.shape[0]
-        high, low = split2(x)
-        both = jnp.concatenate([high, low], axis=0)
+        both = x.astype(BF16)
         both = jnp.concatenate([both[:, wide - LANES :], both, both[:, :LANES]], axis=1)
         parts = []
         for u in range(held // 2):
-            got = dot(both[:, 2 * u * LANES : (2 * u + 4) * LANES], mat[u])
-            parts.append(got[:rows] + got[rows:])
+            parts.append(dot(both[:, 2 * u * LANES : (2 * u + 4) * LANES], mat[u]))
         return degree * x - jnp.concatenate(parts, axis=1)
 
-    def adjoint(x):
-        rows = x.shape[0]
-        high, low = split2(x)
-        both = jnp.concatenate([high, low], axis=0)
+    def adjoint(x, reach):
+        both = x.astype(BF16)
         sums = [None] * held
         for u in range(held // 2):
+            if all(abs(offsets[(2 * u - 1 + i) % held]) > reach for i in range(4)):
+                continue
             got = dot(both[:, 2 * u * LANES : (2 * u + 2) * LANES], mat[u], ((1,), (1,)))
-            got = got[:rows] + got[rows:]
             for i in range(4):
                 s = (2 * u - 1 + i) % held
                 piece = got[:, i * LANES : (i + 1) * LANES]
                 sums[s] = piece if sums[s] is None else sums[s] + piece
-        return degree * x - jnp.concatenate(sums, axis=1)
+        blank = jnp.zeros((x.shape[0], LANES), F32)
+        return degree * x - jnp.concatenate([blank if s is None else s for s in sums], axis=1)
 
     poly = [jnp.concatenate([pg[t] for t in range(held)], axis=1).astype(F32)]
     poly.append(forward(poly[0]))
@@ -271,9 +269,9 @@
     coarse_adj = dot(conv_c[...], coarse_delta)
     adj = [coarse_adj[32 * k : 32 * (k + 1)] for k in range(ORDER)]
     for k in range(ORDER - 1, 1, -1):
-        adj[k - 1] = adj[k - 1] + 2.0 * adjoint(adj[k])
+        adj[k - 1] = adj[k - 1] + 2.0 * adjoint(adj[k], k - 1)
         adj[k - 2] = adj[k - 2] - adj[k]
-    pooled_grad = (adj[0] + adjoint(adj[1]))[:, :LANES] * 0.0625
+    pooled_grad = (adj[0] + adjoint(adj[1], 0))[:, :LANES] * 0.0625
 
     pool_t = ((1,), (1,))
     grad_high, grad_low_part = split2(pooled_grad)

time: 30.1 us -> 29.7 us (0.987)
  Pallas kernels: 29.2 us -> 28.8 us
    pallas_call x1, Pallas kernels: 27.6 us -> 27.2 us  [on_device(): pl.pallas_call(partial(kernel, ring, reps, scale), out_shape=shapes, in_s...]
where the time goes in v4:
time: 29.7 us; the launch traced here: 29.5 us
  Pallas kernels  28.8 us (97%)
  between operations  0.64 us (2%)
    pallas_call x1, Pallas kernels, on_device(): pl.pallas_call(partial(kernel, ring, reps, scale), out_shape=shapes, in_s...  27.2 us
    pallas_call x1, Pallas kernels, on_device(): pl.pallas_call(write_out, out_shape=shapes, in_specs=[hbm] * 4, out_specs...  1.64 us

profile of v4, /device:TPU:0, one launch (start us, length us, event | category | flops | bytes accessed | tf_op | source)
XLA Modules:
  0.0 29.5 jit_solution(13141946483597878626)
XLA Ops:
  0.6 27.2 %unet.1 = (bf16[1,8,2048]{2,1,0:T(8,128)(2,1)}, f32[32,48]{1,0:T(8,128)}, f32[192,128]{1,0:T(8,128)}, f32[8,160]{1,0:T(8,128)}) custom-call(bf16[1,8,2048]{2,1,0:T(8,128)(2,1)} %refs_0_.1, s32[8,2048]{1,0:T(8,128)} %refs_1_.1, f32[8,2048]{1,0:T(8,128)} %refs_2_.1, s32[8,128]{1,0:T(8,128)} %refs_3_.1, f32[8,128]{1,0:T(8,128)} %refs_4_.1, ...), custom_call_target="tpu_custom_call" | custom-call | tf_op jit(solution)/shard_map/unet/pallas_call | solution.py:368
  27.8 1.6 %write_out.1 = (bf16[1,8,2048]{2,1,0:T(8,128)(2,1)}, f32[32,48]{1,0:T(8,128)}, f32[192,128]{1,0:T(8,128)}, f32[8,160]{1,0:T(8,128)}) custom-call(bf16[1,8,2048]{2,1,0:T(8,128)(2,1)} %get-tuple-element.12.refs_0_, f32[32,48]{1,0:T(8,128)} %get-tuple-element.13.refs_1_, f32[192,128]{1,0:T(8,128)} %get-tuple-element.14.refs_2_, f32[8,160]{1,0:T(8,128)} %get-tuple-element.15.refs_3_), custom_call_target="tpu_custom_call" | custom-call | tf_op jit(solution)/shard_map/write_out/pallas_call | solution.py:408
